TPU v7x, 128 devices: a whole 4x4x4 slice. The times are simulated.
128 devices in a mesh: track: 16 (over x, z_lo, core), cross: 8 (over z_hi, y).
Axes of the slice: x: 4, y: 4, z: 4 (z_hi: 2, z_lo: 2; z = z_hi * 2 + z_lo), core: 2. Of those that a mesh axis runs over, the one named last changes fastest.
Arguments:
- order_parameter_field: float32 [8, 512, 256, 128], P(None, 'track', 'cross'), may hold values from 0 to 1
- reduced_warmth_ratio: float32 [128, 512, 256], P(('track', 'cross')), may hold values from 0.6 to 1.4
- entry_crystal_label: int32 [16, 8, 4, 8], P('track', 'cross'), may hold values from 0 to 8191, as said below
- number_of_live_entries: int32 [16, 8, 4], P('track', 'cross'), may hold values from 3 to 8
- boundary_speed_factor: float32 [8192], replicated, may hold values from 0.5 to 2
- heat_sheet_locator: int32 [128], replicated, may hold values from 0 to 127, each once
Outputs:
- new_phases: float32 [8, 512, 256, 128], P(None, 'track', 'cross')
Inputs may be any that keep to these rules, and one draw needn't show every extreme that they name: `entry_crystal_label`: within a block the 8 ids are distinct.
All inputs are finite; a program needn't handle non-finite values.
Results may differ from a plain program's by a relative error of at most 0.0001.
Values sent between devices are 32-bit elements; how exact they have to be, the bound alone decides.
A program may use at most 256 MiB of HBM per device.

v0:
```python
import jax
import jax.numpy as jnp
from jax import lax
from jax.sharding import PartitionSpec as P

STEPS = 2


mixing = 1.5
gradient_coef = 1.0
undercool_gain = 4.0
time_step = 0.06


def padded(cells, sides, width):
    for axis, dim in sides:
        count = lax.axis_size(axis)
        ends = count - 1
        head = lax.slice_in_dim(cells, 0, width, axis=dim)
        tail = lax.slice_in_dim(cells, cells.shape[dim] - width, cells.shape[dim], axis=dim)
        cells = jnp.concatenate(
            [
                lax.ppermute(tail, axis, [(i, (i + 1) % count) for i in range(ends)]),
                cells,
                lax.ppermute(head, axis, [((i + 1) % count, i) for i in range(ends)]),
            ],
            axis=dim,
        )
    return cells


def match_table(own_codes, peer_codes):
    equal_ids = (own_codes[..., :, None] == peer_codes[..., None, :]) & (
        own_codes[..., :, None] > 0
    )
    return equal_ids.astype(jnp.float32)


def remap_face(remap, face):
    slot_count, extent_w, extent_z = face.shape
    blocks = remap.shape[0]
    divided = face.reshape(slot_count, extent_w, blocks, extent_z // blocks)
    carried = jnp.einsum("kst,tykz->sykz", remap, divided, precision=lax.Precision.HIGHEST)
    return carried.reshape(slot_count, extent_w, extent_z)


def advance(field_now, heat_field, mobility_slot, neighbour_faces, remaps, borders):
    slot_count, track_extent, cross_extent, extent_z = field_now.shape
    blocks = mobility_slot.shape[0]
    minus_x = jnp.where(borders[0], field_now[:, 0], remap_face(remaps[0], neighbour_faces[0]))
    plus_x = jnp.where(borders[1], field_now[:, -1], remap_face(remaps[1], neighbour_faces[1]))
    minus_y = jnp.where(borders[2], field_now[:, :, 0], remap_face(remaps[2], neighbour_faces[2]))
    plus_y = jnp.where(borders[3], field_now[:, :, -1], remap_face(remaps[3], neighbour_faces[3]))
    laplace = jnp.concatenate([field_now[:, 1:], plus_x[:, None]], axis=1) + jnp.concatenate(
        [minus_x[:, None], field_now[:, :-1]], axis=1
    )
    laplace = (
        laplace
        + jnp.concatenate([field_now[:, :, 1:], plus_y[:, :, None]], axis=2)
        + jnp.concatenate([minus_y[:, :, None], field_now[:, :, :-1]], axis=2)
    )
    blocked = field_now.reshape(slot_count, track_extent, cross_extent, blocks, extent_z // blocks)
    from_above = jnp.einsum(
        "kst,txyk->sxyk", remaps[4], blocked[:, :, :, 1:, 0], precision=lax.Precision.HIGHEST
    )
    from_below = jnp.einsum(
        "kts,txyk->sxyk", remaps[4], blocked[:, :, :, :-1, -1], precision=lax.Precision.HIGHEST
    )
    upper_rim = jnp.concatenate([from_above, blocked[:, :, :, -1:, -1]], axis=3)
    lower_rim = jnp.concatenate([blocked[:, :, :, :1, 0], from_below], axis=3)
    above = jnp.concatenate([blocked[:, :, :, :, 1:], upper_rim[..., None]], axis=4)
    below = jnp.concatenate([lower_rim[..., None], blocked[:, :, :, :, :-1]], axis=4)
    laplace = laplace + (above + below).reshape(field_now.shape) - 6.0 * field_now
    squares = jnp.sum(field_now * field_now, axis=0)
    undercool = undercool_gain * (1.0 - heat_field)
    mobility_cell = jnp.repeat(mobility_slot.T, extent_z // blocks, axis=1)[:, None, None, :]
    cubed = field_now * field_now * field_now
    change = (
        field_now
        - cubed
        - 2.0 * mixing * field_now * (squares - field_now * field_now)
        + gradient_coef * laplace
        + undercool * field_now * (1.0 - field_now)
    )
    return field_now + time_step * mobility_cell * change


def on_device(
    order_parameter_field,
    reduced_warmth_ratio,
    entry_crystal_label,
    number_of_live_entries,
    boundary_speed_factor,
    heat_sheet_locator,
):
    slot_count, track_extent, cross_extent, extent_z = order_parameter_field.shape
    track_block_count = lax.axis_size("track")
    cross_block_count = lax.axis_size("cross")
    track_pos = lax.axis_index("track")
    cross_pos = lax.axis_index("cross")
    vertical_sheets, scan_tile_lattice, lateral_tile_lattice = reduced_warmth_ratio.shape
    result_fragments = reduced_warmth_ratio.reshape(
        vertical_sheets, track_block_count, track_extent, cross_block_count, cross_extent
    ).transpose(1, 3, 0, 2, 4)
    outgoing = result_fragments.reshape(
        track_block_count * cross_block_count, vertical_sheets, track_extent * cross_extent
    )
    incoming = lax.all_to_all(outgoing, ("track", "cross"), split_axis=0, concat_axis=0, tiled=True)
    inverse = jnp.argsort(heat_sheet_locator)
    placed = jnp.take(incoming, inverse, axis=0).reshape(extent_z, track_extent * cross_extent)
    heat_field = placed.T.reshape(track_extent, cross_extent, extent_z)
    block_ids = entry_crystal_label[0, 0]
    counts = number_of_live_entries[0, 0]
    active = jnp.arange(slot_count, dtype=jnp.int32)[None, :] < counts[:, None]
    mobility_slot = jnp.take(boundary_speed_factor, block_ids, axis=0)
    grain_codes = jnp.where(active, block_ids + 1, 0)
    beside_all = padded(grain_codes[None, None], (("track", 0), ("cross", 1)), 1)
    remaps = (
        match_table(grain_codes, beside_all[0, 1]),
        match_table(grain_codes, beside_all[2, 1]),
        match_table(grain_codes, beside_all[1, 0]),
        match_table(grain_codes, beside_all[1, 2]),
        match_table(grain_codes[:-1], grain_codes[1:]),
    )
    borders = (
        track_pos == 0,
        track_pos == track_block_count - 1,
        cross_pos == 0,
        cross_pos == cross_block_count - 1,
    )
    blocks = block_ids.shape[0]
    live_mask = jnp.repeat(active.T.astype(order_parameter_field.dtype), extent_z // blocks, axis=1)
    field_now = order_parameter_field * live_mask[:, None, None, :]
    for step_index in range(STEPS):
        track_edges = jnp.stack([field_now[:, 0], field_now[:, -1]], axis=1)
        cross_edges = jnp.stack([field_now[:, :, 0], field_now[:, :, -1]], axis=2)
        around_x = padded(track_edges, (("track", 1),), 1)
        around_y = padded(cross_edges, (("cross", 2),), 1)
        neighbour_faces = (around_x[:, 0], around_x[:, 3], around_y[:, :, 0], around_y[:, :, 3])
        field_now = advance(field_now, heat_field, mobility_slot, neighbour_faces, remaps, borders)
    return field_now


def solution(mesh):
    return jax.shard_map(
        on_device,
        mesh=mesh,
        in_specs=(
            P(None, "track", "cross", None),
            P(("track", "cross"), None, None),
            P("track", "cross", None, None),
            P("track", "cross", None),
            P(),
            P(),
        ),
        out_specs=P(None, "track", "cross", None),
        check_vma=False,
    )
```

profile of v0, /device:TPU:25, one launch (start us, length us, event | category | flops | bytes accessed | tf_op | source)
XLA Modules:
  0.0 526.6 jit_solution(7709389187536243376)
XLA Ops:
  28.9 9.6 %all-to-all-start = ((f32[128,1,1024]{2,1,0:T(1,128)}), f32[128,1,1024]{2,1,0:T(1,128)S(1)}, u32[]{:S(2)}, u32[]{:S(2)}) async-start(f32[128,1,1024]{2,1,0:T(1,128)} %reshape.228), calls=%async_computation | async-start | bytes 1048576 | tf_op jit(solution)/shard_map/all_to_all | solution.py:108
  43.3 12.8 %reshape.226 = f32[8,32,32,4,32]{4,3,2,1,0:T(4,128)} reshape(f32[8,32,32,128]{3,2,1,0:T(8,128)} %copy.77) | data formatting | bytes 8388608 | tf_op jit(solution)/shard_map/reshape | solution.py:62
  56.1 30.9 %fusion.88 = (f32[8,32,32,3,1]{4,3,2,1,0:T(4,128)}, f32[8,32,32,3,1]{4,3,2,1,0:T(4,128)}) fusion(f32[8,32,32,4,32]{4,3,2,1,0:T(4,128)} %reshape.226), kind=kLoop, calls=%fused_computation.148 | loop fusion | bytes 393216 | tf_op jit(solution)/shard_map/slice | solution.py:67
  87.0 12.8 %fusion.87 = (f32[8,32,32,1,1]{4,3,2,1,0:T(1,128)}, f32[8,32,32,1,1]{4,3,2,1,0:T(1,128)}) fusion(f32[8,32,32,4,32]{4,3,2,1,0:T(4,128)S(1)} %copy-done.2), kind=kLoop, calls=%fused_computation.147 | loop fusion | bytes 131072 | tf_op jit(solution)/shard_map/slice | solution.py:70
  99.8 14.5 %fusion.89 = (f32[8,32,32,4,31]{4,3,2,1,0:T(4,128)}, f32[8,32,32,4,31]{4,3,2,1,0:T(4,128)}) fusion(f32[8,32,32,4,32]{4,3,2,1,0:T(4,128)S(1)} %copy-done.2), kind=kLoop, calls=%fused_computation.149 | loop fusion | bytes 16252928 | tf_op jit(solution)/shard_map/slice | solution.py:72
  125.8 13.5 %copy.141 = f32[8,32,32,3,1]{2,0,1,3,4:T(8,128)S(1)} copy(f32[8,32,32,3,1]{4,3,2,1,0:T(4,128)} %get-tuple-element.21) | data formatting | bytes 196608
  149.0 11.8 %copy.84 = f32[8,32,32,4,1]{4,3,2,1,0:T(4,128)} copy(f32[8,32,32,4,1]{2,0,1,3,4:T(8,128)S(1)} %maximum_bitcast_fusion.1) | data formatting | bytes 262144 | tf_op jit(solution)/shard_map/broadcast_in_dim | solution.py:72
  160.8 13.5 %copy.138 = f32[8,32,32,3,1]{2,0,1,3,4:T(8,128)S(1)} copy(f32[8,32,32,3,1]{4,3,2,1,0:T(4,128)} %get-tuple-element.22) | data formatting | bytes 196608
  174.7 9.2 %copy.139 = f32[8,32,32,1,1]{2,0,1,4,3:T(8,128)S(1)} copy(f32[8,32,32,1,1]{4,3,2,1,0:T(1,128)} %get-tuple-element.20) | data formatting | bytes 65536
  184.0 11.8 %copy.81 = f32[8,32,32,4,1]{4,3,2,1,0:T(4,128)} copy(f32[8,32,32,4,1]{2,0,1,3,4:T(8,128)S(1)} %maximum_bitcast_fusion) | data formatting | bytes 262144 | tf_op jit(solution)/shard_map/broadcast_in_dim | solution.py:71
  195.8 31.4 %maximum_add_fusion = f32[8,32,32,4,32]{4,3,2,1,0:T(4,128)} fusion(f32[8,32,32,4,1]{4,3,2,1,0:T(4,128)} %copy.81, f32[8,32,32,4,31]{4,3,2,1,0:T(4,128)} %get-tuple-element.24, f32[8,32,32,4,31]{4,3,2,1,0:T(4,128)} %get-tuple-element.23, f32[8,32,32,4,1]{4,3,2,1,0:T(4,128)} %copy.84), kind=kLoop, calls=%fused_computation.2 | loop fusion | flops 3145728 | bytes 12582912 | tf_op jit(solution)/shard_map/add | solution.py:73
  227.2 13.5 %add.115 = f32[8,32,32,128]{3,2,1,0:T(8,128)} reshape(f32[8,32,32,4,32]{4,3,2,1,0:T(4,128)} %maximum_add_fusion) | data formatting | bytes 8388608 | tf_op jit(solution)/shard_map/add | solution.py:73
  272.4 10.7 %multiply_reduce_fusion = (f32[32,32,128]{2,1,0:T(8,128)S(1)}, f32[8,32,32,128]{3,2,0,1:T(8,128)S(1)}) fusion(f32[8,32,32,128]{3,2,0,1:T(8,128)} %copy-done.4, f32[32,32,128]{2,1,0:T(8,128)S(1)} %bitcast.163, f32[8,32,32,128]{3,2,1,0:T(8,128)} %add.115, f32[8,32,31,128]{3,2,0,1:T(8,128)} %get-tuple-element.42, f32[8,32,1,128]{3,2,0,1:T(1,128)S(1)} %get-tuple-element.44, ...), kind=kLoop, calls=%fused_computation.7 | loop fusion | flops 27131904 | bytes 30937088 | tf_op jit(solution)/shard_map/reduce_sum | solution.py:74
  287.4 12.8 %reshape.233 = f32[8,32,32,4,32]{4,3,2,1,0:T(4,128)} reshape(f32[8,32,32,128]{3,2,1,0:T(8,128)} %copy.100) | data formatting | bytes 8388608 | tf_op jit(solution)/shard_map/reshape | solution.py:62
  300.3 30.9 %fusion.85 = (f32[8,32,32,3,1]{4,3,2,1,0:T(4,128)}, f32[8,32,32,3,1]{4,3,2,1,0:T(4,128)}) fusion(f32[8,32,32,4,32]{4,3,2,1,0:T(4,128)} %reshape.233), kind=kLoop, calls=%fused_computation.145 | loop fusion | bytes 393216 | tf_op jit(solution)/shard_map/slice | solution.py:67
  331.2 12.8 %fusion.84 = (f32[8,32,32,1,1]{4,3,2,1,0:T(1,128)}, f32[8,32,32,1,1]{4,3,2,1,0:T(1,128)}) fusion(f32[8,32,32,4,32]{4,3,2,1,0:T(4,128)S(1)} %copy-done.3), kind=kLoop, calls=%fused_computation.144 | loop fusion | bytes 131072 | tf_op jit(solution)/shard_map/slice | solution.py:70
  343.9 14.8 %fusion.86 = (f32[8,32,32,4,31]{4,3,2,1,0:T(4,128)}, f32[8,32,32,4,31]{4,3,2,1,0:T(4,128)}) fusion(f32[8,32,32,4,32]{4,3,2,1,0:T(4,128)S(1)} %copy-done.3), kind=kLoop, calls=%fused_computation.146 | loop fusion | bytes 16252928 | tf_op jit(solution)/shard_map/slice | solution.py:72
  367.8 13.5 %copy.145 = f32[8,32,32,3,1]{2,0,1,3,4:T(8,128)S(1)} copy(f32[8,32,32,3,1]{4,3,2,1,0:T(4,128)} %get-tuple-element.15) | data formatting | bytes 196608
  391.0 11.8 %copy.107 = f32[8,32,32,4,1]{4,3,2,1,0:T(4,128)} copy(f32[8,32,32,4,1]{2,0,1,3,4:T(8,128)S(1)} %maximum_bitcast_fusion.3) | data formatting | bytes 262144 | tf_op jit(solution)/shard_map/broadcast_in_dim | solution.py:72
  402.8 13.5 %copy.142 = f32[8,32,32,3,1]{2,0,1,3,4:T(8,128)S(1)} copy(f32[8,32,32,3,1]{4,3,2,1,0:T(4,128)} %get-tuple-element.16) | data formatting | bytes 196608
  426.1 12.2 %copy.104 = f32[8,32,32,4,1]{4,3,2,1,0:T(4,128)} copy(f32[8,32,32,4,1]{2,0,1,3,4:T(8,128)S(1)} %maximum_bitcast_fusion.2) | data formatting | bytes 262144 | tf_op jit(solution)/shard_map/broadcast_in_dim | solution.py:71
  438.3 31.2 %maximum_add_fusion.1 = f32[8,32,32,4,32]{4,3,2,1,0:T(4,128)} fusion(f32[8,32,32,4,1]{4,3,2,1,0:T(4,128)} %copy.104, f32[8,32,32,4,31]{4,3,2,1,0:T(4,128)} %get-tuple-element.18, f32[8,32,32,4,31]{4,3,2,1,0:T(4,128)} %get-tuple-element.17, f32[8,32,32,4,1]{4,3,2,1,0:T(4,128)} %copy.107), kind=kLoop, calls=%fused_computation.3 | loop fusion | flops 3145728 | bytes 12582912 | tf_op jit(solution)/shard_map/add | solution.py:73
  469.5 13.5 %add.126 = f32[8,32,32,128]{3,2,1,0:T(8,128)} reshape(f32[8,32,32,4,32]{4,3,2,1,0:T(4,128)} %maximum_add_fusion.1) | data formatting | bytes 8388608 | tf_op jit(solution)/shard_map/add | solution.py:73
  513.5 10.5 %fusion.11 = f32[8,32,32,128]{3,2,0,1:T(8,128)S(1)} fusion(f32[8,32,32,128]{3,2,0,1:T(8,128)} %copy-done.6, f32[8,1,32,128]{3,2,0,1:T(8,128)S(1)} %get-tuple-element.30, f32[8,31,32,128]{3,2,0,1:T(8,128)} %get-tuple-element.34, f32[8,31,32,128]{3,2,0,1:T(8,128)} %get-tuple-element.33, f32[8,1,32,128]{3,2,0,1:T(8,128)S(1)} %get-tuple-element.29, ...), kind=kLoop, calls=%fused_computation.21 | loop fusion | flops 25165824 | bytes 30412800 | tf_op jit(solution)/shard_map/add | solution.py:85
  (147 shorter events, 152.3 us)
Async XLA Ops:
  0.0 240.7 %copy-start = (f32[8192]{0:T(1024)S(1)}, f32[8192]{0:T(1024)}, u32[]{:S(2)}) copy-start(f32[8192]{0:T(1024)} %param.10) | copy-start | bytes 98308
  0.8 240.8 %collective-permute-start.1 = (s32[1,1,4,8]{3,2,1,0:T(4,128)S(1)}, s32[1,1,4,8]{3,2,1,0:T(4,128)S(1)}, u32[]{:S(2)}, u32[]{:S(2)}) collective-permute-start(s32[1,1,4,8]{3,2,1,0:T(4,128)S(1)} %add_select_fusion), channel_id=1, source_target_pairs={{8,0},{16,8},{24,16},{32,24},{40,32},{48,40},{56,48},{64,56},{72,6... | collective-permute-start | bytes 392 | tf_op jit(solution)/shard_map/ppermute | solution.py:25
  3.3 241.8 %collective-permute-start.3 = (s32[1,1,4,8]{3,2,1,0:T(4,128)S(1)}, s32[1,1,4,8]{3,2,1,0:T(4,128)S(1)}, u32[]{:S(2)}, u32[]{:S(2)}) collective-permute-start(s32[1,1,4,8]{3,2,1,0:T(4,128)S(1)} %add_select_fusion), channel_id=1, source_target_pairs={{0,8},{8,16},{16,24},{24,32},{32,40},{40,48},{48,56},{56,64},{64,7... | collective-permute-start | bytes 392 | tf_op jit(solution)/shard_map/ppermute | solution.py:23
  7.6 15.7 %copy-start.9 = (f32[1,512,256]{2,1,0:T(8,128)S(1)}, f32[1,512,256]{2,1,0:T(8,128)}, u32[]{:S(2)}) copy-start(f32[1,512,256]{2,1,0:T(8,128)} %param.7) | copy-start | bytes 1572868
  10.7 10.0 %copy-start.4 = (f32[8,32,32,128]{3,2,0,1:T(8,128)}, f32[8,32,32,128]{3,2,0,1:T(8,128)S(1)}, u32[]{:S(2)}) copy-start(f32[8,32,32,128]{3,2,0,1:T(8,128)S(1)} %get-tuple-element.10) | copy-start | bytes 12582916
  11.8 245.7 %collective-permute-start.4 = (f32[8,32,1,128]{3,2,0,1:T(1,128)}, f32[8,32,1,128]{3,2,0,1:T(1,128)}, u32[]{:S(2)}, u32[]{:S(2)}) collective-permute-start(f32[8,32,1,128]{3,2,0,1:T(1,128)} %get-tuple-element.45), channel_id=1, source_target_pairs={{1,0},{2,1},{3,2},{4,3},{5,4},{6,5},{7,6},{9,8},{10,9},{11,10},{12... | collective-permute-start | bytes 393224 | tf_op jit(solution)/shard_map/ppermute | solution.py:25
  14.2 245.9 %collective-permute-start.6 = (f32[8,32,1,128]{3,2,0,1:T(1,128)}, f32[8,32,1,128]{3,2,0,1:T(1,128)}, u32[]{:S(2)}, u32[]{:S(2)}) collective-permute-start(f32[8,32,1,128]{3,2,0,1:T(1,128)} %get-tuple-element.46), channel_id=1, source_target_pairs={{0,1},{1,2},{2,3},{3,4},{4,5},{5,6},{6,7},{8,9},{9,10},{10,11},{11... | collective-permute-start | bytes 393224 | tf_op jit(solution)/shard_map/ppermute | solution.py:23
  21.4 241.5 %collective-permute-start = (f32[8,1,32,128]{3,2,0,1:T(8,128)}, f32[8,1,32,128]{3,2,0,1:T(8,128)S(1)}, u32[]{:S(2)}, u32[]{:S(2)}) collective-permute-start(f32[8,1,32,128]{3,2,0,1:T(8,128)} %get-tuple-element.39), channel_id=1, source_target_pairs={{8,0},{16,8},{24,16},{32,24},{40,32},{48,40},{56,48},{64,56},{72,6... | collective-permute-start | bytes 393224 | tf_op jit(solution)/shard_map/ppermute | solution.py:25
  25.2 13.3 %copy-start.10 = (s32[1,1,4,8]{3,2,1,0:T(4,128)S(1)}, s32[1,1,4,8]{3,2,1,0:T(4,128)}, u32[]{:S(2)}) copy-start(s32[1,1,4,8]{3,2,1,0:T(4,128)} %param.8) | copy-start | bytes 388
  25.2 13.3 %copy-start.11 = (s32[1,1,4]{2,1,0:T(1,128)S(1)}, s32[1,1,4]{2,1,0:T(1,128)}, u32[]{:S(2)}) copy-start(s32[1,1,4]{2,1,0:T(1,128)} %param.9) | copy-start | bytes 52
  28.9 242.2 %all-to-all-start = ((f32[128,1,1024]{2,1,0:T(1,128)}), f32[128,1,1024]{2,1,0:T(1,128)S(1)}, u32[]{:S(2)}, u32[]{:S(2)}) async-start(f32[128,1,1024]{2,1,0:T(1,128)} %reshape.228), calls=%async_computation | async-start | bytes 1048576 | tf_op jit(solution)/shard_map/all_to_all | solution.py:108
  56.1 30.9 %copy-start.2 = (f32[8,32,32,4,32]{4,3,2,1,0:T(4,128)S(1)}, f32[8,32,32,4,32]{4,3,2,1,0:T(4,128)}, u32[]{:S(2)}) copy-start(f32[8,32,32,4,32]{4,3,2,1,0:T(4,128)} %reshape.226) | copy-start | bytes 12582916
  99.8 14.5 %copy-start.5 = (f32[8,32,32,128]{3,2,0,1:T(8,128)S(1)}, f32[8,32,32,128]{3,2,0,1:T(8,128)}, u32[]{:S(2)}) copy-start(f32[8,32,32,128]{3,2,0,1:T(8,128)} %copy-done.4) | copy-start | bytes 12582916
  118.9 4.3 copy-start.12
  241.5 22.3 %collective-permute-start.2 = (f32[8,1,32,128]{3,2,0,1:T(8,128)}, f32[8,1,32,128]{3,2,0,1:T(8,128)S(1)}, u32[]{:S(2)}, u32[]{:S(2)}) collective-permute-start(f32[8,1,32,128]{3,2,0,1:T(8,128)} %get-tuple-element.40), channel_id=1, source_target_pairs={{0,8},{8,16},{16,24},{24,32},{32,40},{40,48},{48,56},{56,64},{64,7... | collective-permute-start | bytes 393224 | tf_op jit(solution)/shard_map/ppermute | solution.py:23
  245.2 8.0 %collective-permute-start.5 = (s32[3,1,4,8]{3,2,1,0:T(4,128)S(1)}, s32[3,1,4,8]{3,2,1,0:T(4,128)S(1)}, u32[]{:S(2)}, u32[]{:S(2)}) collective-permute-start(s32[3,1,4,8]{3,2,1,0:T(4,128)S(1)} %pad_add_fusion), channel_id=1, source_target_pairs={{1,0},{2,1},{3,2},{4,3},{5,4},{6,5},{7,6},{9,8},{10,9},{11,10},{12... | collective-permute-start | bytes 1160 | tf_op jit(solution)/shard_map/ppermute | solution.py:25
  253.2 4.4 collective-permute-start.7
  300.2 30.9 %copy-start.3 = (f32[8,32,32,4,32]{4,3,2,1,0:T(4,128)S(1)}, f32[8,32,32,4,32]{4,3,2,1,0:T(4,128)}, u32[]{:S(2)}) copy-start(f32[8,32,32,4,32]{4,3,2,1,0:T(4,128)} %reshape.233) | copy-start | bytes 12582916
  343.9 14.8 %copy-start.7 = (f32[8,32,32,128]{3,2,0,1:T(8,128)S(1)}, f32[8,32,32,128]{3,2,0,1:T(8,128)}, u32[]{:S(2)}) copy-start(f32[8,32,32,128]{3,2,0,1:T(8,128)} %copy-done.6) | copy-start | bytes 12582916
  482.9 12.8 %collective-permute-start.11 = (f32[8,32,1,128]{3,2,0,1:T(1,128)S(1)}, f32[8,32,1,128]{3,2,0,1:T(1,128)S(1)}, u32[]{:S(2)}, u32[]{:S(2)}) collective-permute-start(f32[8,32,1,128]{3,2,0,1:T(1,128)S(1)} %slice.161), channel_id=1, source_target_pairs={{0,1},{1,2},{2,3},{3,4},{4,5},{5,6},{6,7},{8,9},{9,10},{10,11},{11... | collective-permute-start | bytes 393224 | tf_op jit(solution)/shard_map/ppermute | solution.py:23
  489.5 11.9 %collective-permute-start.8 = (f32[8,1,32,128]{3,2,0,1:T(8,128)S(1)}, f32[8,1,32,128]{3,2,0,1:T(8,128)S(1)}, u32[]{:S(2)}, u32[]{:S(2)}) collective-permute-start(f32[8,1,32,128]{3,2,0,1:T(8,128)S(1)} %get-tuple-element.32), channel_id=1, source_target_pairs={{8,0},{16,8},{24,16},{32,24},{40,32},{48,40},{56,48},{64,56},{72,6... | collective-permute-start | bytes 393224 | tf_op jit(solution)/shard_map/ppermute | solution.py:25
  492.5 10.4 %collective-permute-start.9 = (f32[8,1,32,128]{3,2,0,1:T(8,128)S(1)}, f32[8,1,32,128]{3,2,0,1:T(8,128)S(1)}, u32[]{:S(2)}, u32[]{:S(2)}) collective-permute-start(f32[8,1,32,128]{3,2,0,1:T(8,128)S(1)} %get-tuple-element.31), channel_id=1, source_target_pairs={{0,8},{8,16},{16,24},{24,32},{32,40},{40,48},{48,56},{56,64},{64,7... | collective-permute-start | bytes 393224 | tf_op jit(solution)/shard_map/ppermute | solution.py:23
  499.4 10.4 %collective-permute-start.10 = (f32[8,32,1,128]{3,2,0,1:T(1,128)S(1)}, f32[8,32,1,128]{3,2,0,1:T(1,128)S(1)}, u32[]{:S(2)}, u32[]{:S(2)}) collective-permute-start(f32[8,32,1,128]{3,2,0,1:T(1,128)S(1)} %get-tuple-element.26), channel_id=1, source_target_pairs={{1,0},{2,1},{3,2},{4,3},{5,4},{6,5},{7,6},{9,8},{10,9},{11,10},{12... | collective-permute-start | bytes 393224 | tf_op jit(solution)/shard_map/ppermute | solution.py:25
  513.4 13.0 %copy-start.1 = (f32[8192]{0:T(1024)S(1)}, f32[8192]{0:T(1024)}, u32[]{:S(2)}) copy-start(f32[8192]{0:T(1024)} %param.10) | copy-start | bytes 98308
  (2 other events, 3.7 us)
where the time goes:
time: 533 us; the launch traced here: 527 us
  local copies, waits for them, and re-layouts  356 us (67%)
  other arithmetic  103 us (19%)
  starting transfers between devices  48 us (9%)
  waiting for transfers between devices  12.1 us (2%)
  matrix products  6.75 us (1%)
    unnamed x35, local copies, waits for them, and re-layouts  93.1 us
    add x2, other arithmetic, advance(): above + below  62.6 us
    slice x2, local copies, waits for them, and re-layouts, advance(): blocked[:, :, :, :-1, -1]  61.8 us
    slice x2, local copies, waits for them, and re-layouts, advance(): blocked[:, :, :, :, :-1]  29.4 us
    add x2, local copies, waits for them, and re-layouts, advance(): above + below  26.9 us
    reshape x2, local copies, waits for them, and re-layouts, advance(): field_now.reshape(slot_count, track_extent, cross_extent, blocks, extent_...  25.6 us
    slice x2, local copies, waits for them, and re-layouts, advance(): lower_rim = jnp.concatenate([blocked[:, :, :, :1, 0], from_below], axis=3)  25.6 us
    ppermute x6, starting transfers between devices, padded(): lax.ppermute(tail, axis, [(i, (i + 1) % count) for i in range(ends)])  24.2 us
  transfers between devices with their start and end apart: 13, of which 3 were waited for; matrix products, arithmetic and copies ran while one was open for 45% of the time, Pallas kernels for 0%

commit v1 on v0

v1 whole, which is shorter than its diff:
```python
import functools
import math

import jax
import jax.numpy as jnp
from jax import lax
from jax.experimental import pallas as pl
from jax.experimental.pallas import tpu as pltpu
from jax.sharding import PartitionSpec as P

MIX = 1.5
GRADIENT = 1.0
UNDERCOOL = 4.0
DT = 0.06
ROOT = math.sqrt(2.0)
MESH = pl.DeviceIdType.MESH

S = 8
B = 32
K = 4
Z = B * K
XP = B + 2
YP = B + 16
PLANE = XP * YP


def iota(dim):
    return lax.broadcasted_iota(jnp.int32, (8, Z), dim)


def kernel(
    ntx, nty,
    field_hbm, slab_hbm, label_hbm, count_hbm, speed_hbm, locator_ref,
    out_hbm,
    g0, g1, out, slab, send, recv, u_ref,
    label, count, speed,
    code, code_in, face_y, face_in,
    move, weight, q_idx, q_keep, mob, mm,
    load_sem, heat_send, heat_recv, send_sem, recv_sem, own_sem, out_sem,
):
    nd = ntx * nty
    tx, ty = lax.axis_index("track"), lax.axis_index("cross")
    me = tx * nty + ty
    lane, sub = iota(1), iota(0)

    def load(source, target, index):
        return pltpu.make_async_copy(source, target, load_sem.at[index])

    inner0 = g0.at[:, pl.ds(1, B), pl.ds(8, B), :]
    loads = (
        load(slab_hbm.at[0], slab, 0),
        load(field_hbm, inner0, 1),
        load(label_hbm, label, 2),
        load(count_hbm, count, 3),
        load(speed_hbm, speed, 4),
    )
    loads[0].start()
    barrier = pltpu.get_barrier_semaphore()

    def peers(action):
        def outer(i, carry):
            px = lax.rem(tx + i, ntx)

            def inner(j, carry):
                @pl.when(i + j > 0)
                def _():
                    action(px, lax.rem(ty + j, nty))

                return carry

            return lax.fori_loop(0, nty, inner, carry)

        lax.fori_loop(0, ntx, outer, 0)

    peers(lambda px, py: pl.semaphore_signal(barrier, inc=1, device_id=(px, py), device_id_type=MESH))
    for entry in loads[1:]:
        entry.start()

    loads[0].wait()
    group = lane // B

    def patches(px, carry):
        for half in range(nty * B // Z):
            rows = [slab[pl.ds(px * B + 8 * a, 8), pl.ds(half * Z, Z)] for a in range(4)]
            for q in range(4):
                tile = rows[q] if q == 0 else None
                parts = [rows[a] if a == q else pltpu.roll(rows[a], (B * (a - q)) % Z, axis=1) for a in range(4)]
                tile = parts[0]
                for a in range(1, 4):
                    tile = jnp.where(group == a, parts[a], tile)
                send[px * nty + half * 4 + q] = tile
        return carry

    lax.fori_loop(0, ntx, patches, 0)
    recv[me] = send[me]
    pl.semaphore_wait(barrier, nd - 1)
    peers(
        lambda px, py: pltpu.make_async_remote_copy(
            send.at[px * nty + py], recv.at[me], heat_send, heat_recv, device_id=(px, py), device_id_type=MESH
        ).start()
    )

    loads[2].wait()
    loads[3].wait()
    loads[4].wait()
    own_code = jnp.zeros((8, Z), jnp.int32)
    mobility = jnp.zeros((8, Z), jnp.float32)
    codes = []
    for k in range(K):
        row = []
        for s in range(S):
            grain = label[k * S + s]
            live = jnp.where(s < count[k], grain + 1, 0)
            row.append(live)
            here = (sub == s) & (group == k)
            own_code = jnp.where(here, live, own_code)
            mobility = jnp.where(here, speed[grain], mobility)
        codes.append(row)
    code[...] = own_code
    mob[...] = DT * mobility
    for s in range(S):
        mm[s] = jnp.broadcast_to(mob[pl.ds(s, 1), :], (8, Z))

    place = lax.rem(lane + 1, B)
    b = lax.rem(place, 2)
    slot_at = place // 2
    kk = (lane + 1) // B
    kk = jnp.where(kk == K, 0, kk)
    own_block = kk - 1 + b
    peer_block = kk - b
    have = jnp.zeros((8, Z), jnp.int32)
    for k in range(K):
        for s in range(S):
            have = jnp.where((own_block == k) & (slot_at == s), codes[k][s], have)
    index = jnp.zeros((8, Z), jnp.int32)
    keep = jnp.zeros((8, Z), jnp.float32)
    for s in range(S):
        other = jnp.zeros((8, Z), jnp.int32)
        for k in range(K):
            other = jnp.where(peer_block == k, codes[k][s], other)
        same = (other == have) & (have > 0)
        index = jnp.where(same, kk * B - b + 2 * s, index)
        keep = jnp.where(same, 1.0, keep)
    index = jnp.where(kk == 0, lane, index)
    keep = jnp.where(kk == 0, 1.0, keep)
    q_idx[...] = index
    q_keep[...] = keep

    zero = jnp.zeros((8, Z), jnp.float32)

    def clear(x, carry):
        for s in range(S):
            for g in (g0, g1):
                g[s, x, pl.ds(0, 8), :] = zero
                g[s, x, pl.ds(YP - 8, 8), :] = zero
        return carry

    lax.fori_loop(0, XP, clear, 0)
    for s in range(S):
        for g in (g0, g1):
            for x in (0, XP - 1):
                for j in range(4):
                    g[s, x, pl.ds(8 + 8 * j, 8), :] = zero
    loads[1].wait()
    scale = [
        jnp.where(jnp.broadcast_to(code[pl.ds(s, 1), :], (8, Z)) > 0, ROOT, 0.0) for s in range(S)
    ]

    def live_only(x, carry):
        for s in range(S):
            for j in range(4):
                at = (s, x, pl.ds(8 + 8 * j, 8), slice(None))
                g0[at] = g0[at] * scale[s]
        return carry

    lax.fori_loop(1, B + 1, live_only, 0)

    lower_x, upper_x = jnp.maximum(tx - 1, 0), jnp.minimum(tx + 1, ntx - 1)
    lower_y, upper_y = jnp.maximum(ty - 1, 0), jnp.minimum(ty + 1, nty - 1)
    at_end = (tx == 0, tx == ntx - 1, ty == 0, ty == nty - 1)
    target = ((lower_x, ty), (upper_x, ty), (tx, lower_y), (tx, upper_y))

    def pack_y(g, step):
        flat = g.reshape(S * PLANE, Z)

        def one(s, carry):
            for side, row in ((0, 8), (1, 8 + B - 1)):
                for x in range(0, B, 8):
                    value = flat[pl.ds(s * PLANE + (x + 1) * YP + row, 8, stride=YP), :]
                    face_y[step, side, s, pl.ds(x, 8), :] = value
            return carry

        lax.fori_loop(0, S, one, 0)

    def face(g, step, f):
        if f < 2:
            return g.at[:, (1, B)[f], pl.ds(8, B), :]
        return face_y.at[step, f - 2]

    def exchange(g, step, f):
        source, sem = face(g, step, f), step * 4 + f
        remote = pltpu.make_async_remote_copy(
            source, face_in.at[step, f ^ 1], send_sem.at[sem], recv_sem.at[sem ^ 1],
            device_id=target[f], device_id_type=MESH,
        )
        local = pltpu.make_async_copy(source, face_in.at[step, f], own_sem.at[sem])
        return remote, local

    def exchange_code(f):
        sem = 8 + f
        remote = pltpu.make_async_remote_copy(
            code, code_in.at[f ^ 1], send_sem.at[sem], recv_sem.at[sem ^ 1],
            device_id=target[f], device_id_type=MESH,
        )
        local = pltpu.make_async_copy(code, code_in.at[f], own_sem.at[sem])
        return remote, local

    def begin(pair, f):
        @pl.when(jnp.logical_not(at_end[f]))
        def _():
            pair[0].start()

        @pl.when(at_end[f])
        def _():
            pair[1].start()

    def finish(pair_sent, pair_got, f):
        @pl.when(jnp.logical_not(at_end[f]))
        def _():
            pair_sent[0].wait_send()
            pair_got[0].wait_recv()

        @pl.when(at_end[f])
        def _():
            pair_sent[1].wait()

    pack_y(g0, 0)
    for f in range(4):
        begin(exchange_code(f), f)
        begin(exchange(g0, 0, f), f)

    rim_low = lax.rem(lane, B) == 0
    rim_high = lax.rem(lane, B) == B - 1
    in_pack = [slot_at == s for s in range(S)]

    def neighbours(g, x, j):
        row = 8 + 8 * j
        own = [g[s, x, pl.ds(row, 8), :] for s in range(S)]
        squares = own[0] * own[0]
        packed = own[0]
        for s in range(1, S):
            squares = squares + own[s] * own[s]
            packed = jnp.where(in_pack[s], pltpu.roll(own[s], 2 * s, axis=1), packed)
        rim = jnp.take_along_axis(packed, q_idx[...], axis=1) * q_keep[...]
        sums = []
        for s in range(S):
            back = rim if s == 0 else pltpu.roll(rim, Z - 2 * s, axis=1)
            below = jnp.where(rim_low, back, pltpu.roll(own[s], 1, axis=1))
            above = jnp.where(rim_high, back, pltpu.roll(own[s], Z - 1, axis=1))
            total = g[s, x - 1, pl.ds(row, 8), :] + g[s, x + 1, pl.ds(row, 8), :]
            total = total + (g[s, x, pl.ds(row - 1, 8), :] + g[s, x, pl.ds(row + 1, 8), :])
            sums.append(total + (below + above))
        return own, squares, sums

    def first_sweep(x, carry):
        for j in range(4):
            own, squares, sums = neighbours(g0, x, j)
            level = (1.0 - 6.0 * GRADIENT) - MIX * squares
            for s in range(S):
                change = own[s] * (level + own[s] * own[s]) + sums[s]
                g1[s, x, pl.ds(8 + 8 * j, 8), :] = own[s] + mm[s] * change
        return carry

    lax.fori_loop(1, B + 1, first_sweep, 0)

    for f in range(4):
        finish(exchange_code(f), exchange_code(f ^ 1), f)
        index = jnp.zeros((8, Z), jnp.int32)
        value = jnp.zeros((8, Z), jnp.float32)
        own_now = code[...]
        for s in range(S):
            other = jnp.broadcast_to(code_in[f, pl.ds(s, 1), :], (8, Z))
            same = (other == own_now) & (own_now > 0)
            index = jnp.where(same, s, index)
            value = jnp.where(same, mob[...], value)
        move[f] = index
        weight[f] = value

    def add_faces(g, base, stride_s, stride_x, first_x, first_y, step, factor, f):
        finish(exchange(g, step, f), exchange(g, step, f ^ 1), f)
        flat = base.reshape(S * stride_s, Z)
        source = face_in.at[step, f].reshape(S * B, Z)
        turn, gain = move[f], weight[f] * factor

        def one(i, carry):
            got = jnp.take_along_axis(source[pl.ds(i, 8, stride=B), :], turn, axis=0)
            if f < 2:
                row = (first_x + (0, B - 1)[f]) * stride_x + first_y + i
            else:
                row = (first_x + i) * stride_x + first_y + (0, B - 1)[f - 2]
            at = (pl.ds(row, 8, stride=stride_s), slice(None))
            flat[at] = flat[at] + gain * got
            return carry

        lax.fori_loop(0, B, one, 0, unroll=4)

    for f in range(4):
        add_faces(g0, g1, PLANE, YP, 1, 8, 0, 1.0, f)

    everyone = pltpu.make_async_remote_copy(
        send.at[pl.ds(0, nd - 1)], recv.at[pl.ds(0, nd - 1)], heat_send, heat_recv,
        device_id=(tx, ty), device_id_type=MESH,
    )
    everyone.wait_send()
    everyone.wait_recv()
    locator = jnp.broadcast_to(locator_ref[...], (Z, Z))
    order = jnp.where(locator == lax.broadcasted_iota(jnp.int32, (Z, Z), 0), 1.0, 0.0).astype(jnp.bfloat16)
    flat_recv = recv.reshape(nd * 8, Z)
    for s in range(8):
        value = (UNDERCOOL / ROOT) * (1.0 - flat_recv[pl.ds(s, nd, stride=8), :])
        value = jnp.transpose(value)
        high = value.astype(jnp.bfloat16)
        low = (value - high.astype(jnp.float32)).astype(jnp.bfloat16)
        dims = (((1,), (1,)), ((), ()))
        placed = lax.dot_general(high, order, dims, preferred_element_type=jnp.float32)
        placed = placed + lax.dot_general(low, order, dims, preferred_element_type=jnp.float32)
        for a in range(4):
            u_ref[pl.ds((8 * a + s) * B, B), :] = placed[a * B : (a + 1) * B]

    def heat_term(x, tiles):
        for j in tiles:
            u = u_ref[pl.ds((x - 1) * B + 8 * j, 8), :]
            for s in range(S):
                at = (s, x, pl.ds(8 + 8 * j, 8), slice(None))
                own = g0[at]
                g1[at] = g1[at] + (mm[s] * u) * (own * (ROOT - own))

    def heat_loop(tiles):
        def body(x, carry):
            heat_term(x, tiles)
            return carry

        lax.fori_loop(2, B, body, 0)

    heat_term(1, range(4))
    heat_term(B, range(4))
    for f in (0, 1):
        begin(exchange(g1, 1, f), f)
    heat_loop((0, 3))
    pack_y(g1, 1)
    for f in (2, 3):
        begin(exchange(g1, 1, f), f)
    heat_loop((1, 2))

    def second_sweep(x, carry):
        for j in range(4):
            own, squares, sums = neighbours(g1, x, j)
            u = u_ref[pl.ds((x - 1) * B + 8 * j, 8), :]
            level = (1.0 - 6.0 * GRADIENT) + ROOT * u - MIX * squares
            for s in range(S):
                change = own[s] * (level + own[s] * (own[s] - u)) + sums[s]
                out[s, x - 1, pl.ds(8 * j, 8), :] = (1.0 / ROOT) * (own[s] + mm[s] * change)
        return carry

    lax.fori_loop(1, B + 1, second_sweep, 0)
    for f in range(4):
        add_faces(g1, out, B * B, B, 0, 0, 1, 1.0 / ROOT, f)
    store = pltpu.make_async_copy(out, out_hbm, out_sem)
    store.start()
    store.wait()


def on_device(ntx, nty, field, heat, label, count, speed, locator):
    nd = ntx * nty
    any_space = pl.BlockSpec(memory_space=pl.ANY)
    return pl.pallas_call(
        functools.partial(kernel, ntx, nty),
        out_shape=jax.ShapeDtypeStruct(field.shape, jnp.float32),
        in_specs=[any_space] * 5 + [pl.BlockSpec(memory_space=pltpu.VMEM)],
        out_specs=any_space,
        scratch_shapes=[
            pltpu.VMEM((S, XP, YP, Z), jnp.float32),
            pltpu.VMEM((S, XP, YP, Z), jnp.float32),
            pltpu.VMEM((S, B, B, Z), jnp.float32),
            pltpu.VMEM(heat.shape[1:], jnp.float32),
            pltpu.VMEM((nd, 8, Z), jnp.float32),
            pltpu.VMEM((nd, 8, Z), jnp.float32),
            pltpu.VMEM((B * B, Z), jnp.float32),
            pltpu.SMEM((K * S,), jnp.int32),
            pltpu.SMEM((K,), jnp.int32),
            pltpu.SMEM(speed.shape, jnp.float32),
            pltpu.VMEM((8, Z), jnp.int32),
            pltpu.VMEM((4, 8, Z), jnp.int32),
            pltpu.VMEM((2, 2, S, B, Z), jnp.float32),
            pltpu.VMEM((2, 4, S, B, Z), jnp.float32),
            pltpu.VMEM((4, 8, Z), jnp.int32),
            pltpu.VMEM((4, 8, Z), jnp.float32),
            pltpu.VMEM((8, Z), jnp.int32),
            pltpu.VMEM((8, Z), jnp.float32),
            pltpu.VMEM((8, Z), jnp.float32),
            pltpu.VMEM((S, 8, Z), jnp.float32),
            pltpu.SemaphoreType.DMA((5,)),
            pltpu.SemaphoreType.DMA,
            pltpu.SemaphoreType.DMA,
            pltpu.SemaphoreType.DMA((12,)),
            pltpu.SemaphoreType.DMA((12,)),
            pltpu.SemaphoreType.DMA((12,)),
            pltpu.SemaphoreType.DMA,
        ],
        compiler_params=pltpu.CompilerParams(
            collective_id=0, has_side_effects=True, vmem_limit_bytes=60 * 2**20
        ),
        name="grains",
    )(
        field,
        heat,
        label.reshape(K * S),
        count.reshape(K),
        speed,
        locator.reshape(1, Z),
    )


def solution(mesh):
    ntx, nty = mesh.shape["track"], mesh.shape["cross"]
    return jax.shard_map(
        functools.partial(on_device, ntx, nty),
        mesh=mesh,
        in_specs=(
            P(None, "track", "cross", None),
            P(("track", "cross"), None, None),
            P("track", "cross", None, None),
            P("track", "cross", None),
            P(),
            P(),
        ),
        out_specs=P(None, "track", "cross", None),
        check_vma=False,
    )
```

time: 533 us -> 45.4 us (0.09)
  the two profiles are of different devices: /device:TPU:25 before, /device:TPU:1 now
where the time goes in v1:
time: 45.4 us; the launch traced here: 45.2 us
  Pallas kernels  39.3 us (87%)
  local copies, waits for them, and re-layouts  5.91 us (13%)
    pallas_call x1, Pallas kernels, on_device(): pl.pallas_call(functools.partial(kernel, ntx, nty), out_shape=jax.ShapeDt...  39.3 us
    unnamed x1, local copies, waits for them, and re-layouts  4.64 us
    reshape x1, local copies, waits for them, and re-layouts, on_device(): label.reshape(K * S)  1.27 us

profile of v1, /device:TPU:1, one launch (start us, length us, event | category | flops | bytes accessed | tf_op | source)
XLA Modules:
  0.0 45.2 jit_solution(13432750408277297030)
XLA Ops:
  0.0 1.3 %reshape.9.label_hbm = s32[32]{0:T(128)} reshape(s32[1,1,4,8]{3,2,1,0:T(4,128)} %param.8) | data formatting | bytes 256 | tf_op jit(solution)/shard_map/reshape | solution.py:417
  1.3 39.3 %grains.1 = f32[8,32,32,128]{3,2,1,0:T(8,128)} custom-call(f32[8,32,32,128]{3,2,1,0:T(8,128)} %field_hbm.1, f32[1,512,256]{2,1,0:T(8,128)} %slab_hbm.1, s32[32]{0:T(128)} %reshape.9.label_hbm, s32[4]{0:T(128)} %bitcast.2, f32[8192]{0:T(1024)} %speed_hbm.1, s32[1,128]{1,0:T(1,128)} %bitcast.3), custom_call_target="tpu_custom_call" | custom-call | tf_op jit(solution)/shard_map/grains/pallas_call | solution.py:376
  40.6 4.6 %copy.8 = f32[8,32,32,128]{3,2,1,0:T(8,128)} copy(f32[8,32,32,128]{3,2,1,0:T(8,128)} %grains.1) | data formatting | bytes 8388608

commit v2 on v1

--- a/solution.py
+++ b/solution.py
@@ -22,6 +22,8 @@
 XP = B + 2
 YP = B + 16
 PLANE = XP * YP
+PIECE = 2
+CHUNK = 8
 
 
 def iota(dim):
@@ -30,13 +32,13 @@
 
 def kernel(
     ntx, nty,
-    field_hbm, slab_hbm, label_hbm, count_hbm, speed_hbm, locator_ref,
-    out_hbm,
-    g0, g1, out, slab, send, recv, u_ref,
-    label, count, speed,
+    field_hbm, slab_hbm, label_hbm, count_hbm, speed_hbm, locator_hbm,
+    out, order_out,
+    raw, g0, g1, slab, send, recv, u_ref, split, couple,
+    label, count, speed, locator_ref,
     code, code_in, face_y, face_in,
-    move, weight, q_idx, q_keep, mob, mm,
-    load_sem, heat_send, heat_recv, send_sem, recv_sem, own_sem, out_sem,
+    move, weight, mob, mm,
+    load_sem, heat_send, heat_recv, send_sem, recv_sem, own_sem,
 ):
     nd = ntx * nty
     tx, ty = lax.axis_index("track"), lax.axis_index("cross")
@@ -46,13 +48,13 @@
     def load(source, target, index):
         return pltpu.make_async_copy(source, target, load_sem.at[index])
 
-    inner0 = g0.at[:, pl.ds(1, B), pl.ds(8, B), :]
     loads = (
         load(slab_hbm.at[0], slab, 0),
-        load(field_hbm, inner0, 1),
+        load(field_hbm, raw, 1),
         load(label_hbm, label, 2),
         load(count_hbm, count, 3),
         load(speed_hbm, speed, 4),
+        load(locator_hbm, locator_ref, 5),
     )
     loads[0].start()
     barrier = pltpu.get_barrier_semaphore()
@@ -103,48 +105,70 @@
     loads[2].wait()
     loads[3].wait()
     loads[4].wait()
+    loads[5].wait()
+    codes, orders, matches = [], [], []
+    for k in range(K):
+        live = [jnp.where(s < count[0, 0, k], label[0, 0, k, s] + 1, 0) for s in range(S)]
+        if k == 0:
+            order, code_at, matched = [jnp.int32(s) for s in range(S)], live, None
+        else:
+            bits = []
+            for j in range(S):
+                bit = jnp.int32(0)
+                for p in range(S):
+                    bit = jnp.where((live[j] == codes[k - 1][p]) & (live[j] > 0), 1 << p, bit)
+                bits.append(bit)
+            matched = functools.reduce(jnp.bitwise_or, bits)
+            free = matched ^ (2**S - 1)
+            for j in range(S):
+                low = free & -free
+                free = jnp.where(bits[j] == 0, free ^ low, free)
+                bits[j] = jnp.where(bits[j] == 0, low, bits[j])
+            order, code_at = [], []
+            for p in range(S):
+                slot, here = jnp.int32(0), live[0]
+                for j in range(1, S):
+                    slot = jnp.where(bits[j] == 1 << p, j, slot)
+                    here = jnp.where(bits[j] == 1 << p, live[j], here)
+                order.append(slot)
+                code_at.append(here)
+            for j in range(S):
+                place = jnp.int32(0)
+                for p in range(1, S):
+                    place = jnp.where(bits[j] == 1 << p, p, place)
+                order_out[k, j] = place
+        if k == 0:
+            for j in range(S):
+                order_out[k, j] = j
+        codes.append(code_at)
+        orders.append(order)
+        matches.append(matched)
     own_code = jnp.zeros((8, Z), jnp.int32)
     mobility = jnp.zeros((8, Z), jnp.float32)
-    codes = []
     for k in range(K):
-        row = []
-        for s in range(S):
-            grain = label[k * S + s]
-            live = jnp.where(s < count[k], grain + 1, 0)
-            row.append(live)
+        for s in range(S):
             here = (sub == s) & (group == k)
-            own_code = jnp.where(here, live, own_code)
-            mobility = jnp.where(here, speed[grain], mobility)
-        codes.append(row)
+            own_code = jnp.where(here, codes[k][s], own_code)
+            mobility = jnp.where(here, speed[label[0, 0, k, orders[k][s]]], mobility)
     code[...] = own_code
     mob[...] = DT * mobility
     for s in range(S):
         mm[s] = jnp.broadcast_to(mob[pl.ds(s, 1), :], (8, Z))
 
-    place = lax.rem(lane + 1, B)
-    b = lax.rem(place, 2)
-    slot_at = place // 2
-    kk = (lane + 1) // B
-    kk = jnp.where(kk == K, 0, kk)
-    own_block = kk - 1 + b
-    peer_block = kk - b
-    have = jnp.zeros((8, Z), jnp.int32)
-    for k in range(K):
-        for s in range(S):
-            have = jnp.where((own_block == k) & (slot_at == s), codes[k][s], have)
-    index = jnp.zeros((8, Z), jnp.int32)
-    keep = jnp.zeros((8, Z), jnp.float32)
+    wide = lax.broadcasted_iota(jnp.int32, (Z, Z), 1)
+    deep = lax.broadcasted_iota(jnp.int32, (Z, Z), 0)
+    beside = (deep == wide - 1) | (deep == wide + 1) | ((deep == wide) & ((wide == 0) | (wide == Z - 1)))
+    edge = jnp.maximum(deep, wide)
+    crossing = (deep != wide) & (lax.rem(edge, B) == 0)
+    base_matrix = jnp.where(beside & jnp.logical_not(crossing), 1.0, 0.0)
+    crossings = [jnp.where(beside & crossing & (edge == k * B), 1.0, 0.0) for k in range(1, K)]
     for s in range(S):
-        other = jnp.zeros((8, Z), jnp.int32)
-        for k in range(K):
-            other = jnp.where(peer_block == k, codes[k][s], other)
-        same = (other == have) & (have > 0)
-        index = jnp.where(same, kk * B - b + 2 * s, index)
-        keep = jnp.where(same, 1.0, keep)
-    index = jnp.where(kk == 0, lane, index)
-    keep = jnp.where(kk == 0, 1.0, keep)
-    q_idx[...] = index
-    q_keep[...] = keep
+        matrix = base_matrix
+        for k in range(1, K):
+            matrix = matrix + jnp.where((matches[k] & (1 << s)) > 0, crossings[k - 1], 0.0)
+        matrix = matrix.astype(jnp.bfloat16)
+        couple[s, pl.ds(0, Z), :] = matrix
+        couple[s, pl.ds(Z, Z), :] = matrix
 
     zero = jnp.zeros((8, Z), jnp.float32)
 
@@ -162,18 +186,29 @@
                 for j in range(4):
                     g[s, x, pl.ds(8 + 8 * j, 8), :] = zero
     loads[1].wait()
+    wide_group = lax.broadcasted_iota(jnp.int32, (16, Z), 1) // B
     scale = [
-        jnp.where(jnp.broadcast_to(code[pl.ds(s, 1), :], (8, Z)) > 0, ROOT, 0.0) for s in range(S)
+        jnp.where(jnp.broadcast_to(code[pl.ds(s, 1), :], (16, Z)) > 0, ROOT, 0.0) for s in range(S)
     ]
 
-    def live_only(x, carry):
-        for s in range(S):
-            for j in range(4):
-                at = (s, x, pl.ds(8 + 8 * j, 8), slice(None))
-                g0[at] = g0[at] * scale[s]
-        return carry
-
-    lax.fori_loop(1, B + 1, live_only, 0)
+    def keep_split(s, row, value):
+        high = value.astype(jnp.bfloat16)
+        split[s, pl.ds(row, 16), pl.ds(0, Z)] = high
+        split[s, pl.ds(row, 16), pl.ds(Z, Z)] = (value - high.astype(jnp.float32)).astype(jnp.bfloat16)
+
+    def place_field(x, carry):
+        for s in range(S):
+            for j in range(0, 4, 2):
+                rows = pl.ds(8 * j, 16)
+                value = raw[s, x, rows, :]
+                for k in range(1, K):
+                    value = jnp.where(wide_group == k, raw[orders[k][s], x, rows, :], value)
+                value = value * scale[s]
+                g0[s, x + 1, pl.ds(8 + 8 * j, 16), :] = value
+                keep_split(s, pl.multiple_of(x * B, B) + 8 * j, value)
+        return carry
+
+    lax.fori_loop(0, B, place_field, 0)
 
     lower_x, upper_x = jnp.maximum(tx - 1, 0), jnp.minimum(tx + 1, ntx - 1)
     lower_y, upper_y = jnp.maximum(ty - 1, 0), jnp.minimum(ty + 1, nty - 1)
@@ -239,39 +274,40 @@
         begin(exchange_code(f), f)
         begin(exchange(g0, 0, f), f)
 
-    rim_low = lax.rem(lane, B) == 0
-    rim_high = lax.rem(lane, B) == B - 1
-    in_pack = [slot_at == s for s in range(S)]
-
-    def neighbours(g, x, j):
-        row = 8 + 8 * j
-        own = [g[s, x, pl.ds(row, 8), :] for s in range(S)]
-        squares = own[0] * own[0]
-        packed = own[0]
-        for s in range(1, S):
-            squares = squares + own[s] * own[s]
-            packed = jnp.where(in_pack[s], pltpu.roll(own[s], 2 * s, axis=1), packed)
-        rim = jnp.take_along_axis(packed, q_idx[...], axis=1) * q_keep[...]
-        sums = []
-        for s in range(S):
-            back = rim if s == 0 else pltpu.roll(rim, Z - 2 * s, axis=1)
-            below = jnp.where(rim_low, back, pltpu.roll(own[s], 1, axis=1))
-            above = jnp.where(rim_high, back, pltpu.roll(own[s], Z - 1, axis=1))
-            total = g[s, x - 1, pl.ds(row, 8), :] + g[s, x + 1, pl.ds(row, 8), :]
-            total = total + (g[s, x, pl.ds(row - 1, 8), :] + g[s, x, pl.ds(row + 1, 8), :])
-            sums.append(total + (below + above))
-        return own, squares, sums
-
-    def first_sweep(x, carry):
-        for j in range(4):
-            own, squares, sums = neighbours(g0, x, j)
-            level = (1.0 - 6.0 * GRADIENT) - MIX * squares
-            for s in range(S):
-                change = own[s] * (level + own[s] * own[s]) + sums[s]
-                g1[s, x, pl.ds(8 + 8 * j, 8), :] = own[s] + mm[s] * change
-        return carry
-
-    lax.fori_loop(1, B + 1, first_sweep, 0)
+    def sweep(g, i, use):
+        rows = pl.ds(pl.multiple_of(i * CHUNK * B, CHUNK * B), CHUNK * B)
+        depth = [
+            lax.dot_general(
+                split[s, rows, :], couple[s], (((1,), (0,)), ((), ())), preferred_element_type=jnp.float32
+            )
+            for s in range(S)
+        ]
+        for part in range(CHUNK):
+            x = i * CHUNK + part + 1
+            for j in range(4):
+                row = 8 + 8 * j
+                own = [g[s, x, pl.ds(row, 8), :] for s in range(S)]
+                squares = own[0] * own[0]
+                for s in range(1, S):
+                    squares = squares + own[s] * own[s]
+                sums = []
+                for s in range(S):
+                    total = g[s, x - 1, pl.ds(row, 8), :] + g[s, x + 1, pl.ds(row, 8), :]
+                    total = total + (g[s, x, pl.ds(row - 1, 8), :] + g[s, x, pl.ds(row + 1, 8), :])
+                    sums.append(total + depth[s][part * B + 8 * j : part * B + 8 * j + 8])
+                use(x, j, own, squares, sums)
+
+    def first(x, j, own, squares, sums):
+        level = (1.0 - 6.0 * GRADIENT) - MIX * squares
+        for s in range(S):
+            change = own[s] * (level + own[s] * own[s]) + sums[s]
+            g1[s, x, pl.ds(8 + 8 * j, 8), :] = own[s] + mm[s] * change
+
+    def first_sweep(i, carry):
+        sweep(g0, i, first)
+        return carry
+
+    lax.fori_loop(0, B // CHUNK, first_sweep, 0)
 
     for f in range(4):
         finish(exchange_code(f), exchange_code(f ^ 1), f)
@@ -327,98 +363,133 @@
         for a in range(4):
             u_ref[pl.ds((8 * a + s) * B, B), :] = placed[a * B : (a + 1) * B]
 
-    def heat_term(x, tiles):
-        for j in tiles:
-            u = u_ref[pl.ds((x - 1) * B + 8 * j, 8), :]
+    def heat_term(x, pairs):
+        for j in pairs:
+            u = u_ref[pl.ds((x - 1) * B + 8 * j, 16), :]
             for s in range(S):
-                at = (s, x, pl.ds(8 + 8 * j, 8), slice(None))
+                at = (s, x, pl.ds(8 + 8 * j, 16), slice(None))
                 own = g0[at]
-                g1[at] = g1[at] + (mm[s] * u) * (own * (ROOT - own))
-
-    def heat_loop(tiles):
-        def body(x, carry):
-            heat_term(x, tiles)
-            return carry
-
-        lax.fori_loop(2, B, body, 0)
-
-    heat_term(1, range(4))
-    heat_term(B, range(4))
+                gain = jnp.concatenate([mm[s], mm[s]], axis=0)
+                value = g1[at] + (gain * u) * (own * (ROOT - own))
+                g1[at] = value
+                keep_split(s, pl.multiple_of((x - 1) * B, B) + 8 * j, value)
+
+    heat_term(1, (0, 2))
+    heat_term(B, (0, 2))
     for f in (0, 1):
         begin(exchange(g1, 1, f), f)
-    heat_loop((0, 3))
+
+    def heat_rest(x, carry):
+        heat_term(x, (0, 2))
+        return carry
+
+    lax.fori_loop(2, B, heat_rest, 0)
     pack_y(g1, 1)
     for f in (2, 3):
         begin(exchange(g1, 1, f), f)
-    heat_loop((1, 2))
-
-    def second_sweep(x, carry):
-        for j in range(4):
-            own, squares, sums = neighbours(g1, x, j)
-            u = u_ref[pl.ds((x - 1) * B + 8 * j, 8), :]
-            level = (1.0 - 6.0 * GRADIENT) + ROOT * u - MIX * squares
-            for s in range(S):
-                change = own[s] * (level + own[s] * (own[s] - u)) + sums[s]
-                out[s, x - 1, pl.ds(8 * j, 8), :] = (1.0 / ROOT) * (own[s] + mm[s] * change)
-        return carry
-
-    lax.fori_loop(1, B + 1, second_sweep, 0)
+
+    def second(x, j, own, squares, sums):
+        u = u_ref[pl.ds((x - 1) * B + 8 * j, 8), :]
+        level = (1.0 - 6.0 * GRADIENT) + ROOT * u - MIX * squares
+        for s in range(S):
+            change = own[s] * (level + own[s] * (own[s] - u)) + sums[s]
+            out[s, x - 1, pl.ds(8 * j, 8), :] = own[s] + mm[s] * change
+
+    def second_sweep(i, carry):
+        sweep(g1, i, second)
+        return carry
+
+    lax.fori_loop(0, B // CHUNK, second_sweep, 0)
     for f in range(4):
-        add_faces(g1, out, B * B, B, 0, 0, 1, 1.0 / ROOT, f)
-    store = pltpu.make_async_copy(out, out_hbm, out_sem)
-    store.start()
-    store.wait()
+        add_faces(g1, out, B * B, B, 0, 0, 1, 1.0, f)
+
+
+def restore(order, moved, result_hbm, result, out_sem):
+    group = lax.broadcasted_iota(jnp.int32, (8, Z), 1) // B
+    places = [[order[k, s] for s in range(S)] for k in range(K)]
+
+    def piece(i):
+        planes = pl.ds(i * PIECE, PIECE)
+        return pltpu.make_async_copy(result.at[:, planes], result_hbm.at[:, planes], out_sem)
+
+    def plane(x):
+        values = []
+        for s in range(S):
+            for j in range(4):
+                rows = pl.ds(8 * j, 8)
+                value = moved[s, x, rows, :]
+                for k in range(1, K):
+                    value = jnp.where(group == k, moved[places[k][s], x, rows, :], value)
+                values.append(value * (1.0 / ROOT))
+        for s in range(S):
+            for j in range(4):
+                result[s, x, pl.ds(8 * j, 8), :] = values[4 * s + j]
+
+    def one(i, carry):
+        for x in range(PIECE):
+            plane(i * PIECE + x)
+        piece(i).start()
+        return carry
+
+    lax.fori_loop(0, B // PIECE, one, 0)
+    pltpu.make_async_copy(result, result_hbm, out_sem).wait()
 
 
 def on_device(ntx, nty, field, heat, label, count, speed, locator):
     nd = ntx * nty
-    any_space = pl.BlockSpec(memory_space=pl.ANY)
-    return pl.pallas_call(
+    in_hbm = pl.BlockSpec(memory_space=pltpu.HBM)
+    f32, i32 = jnp.float32, jnp.int32
+    moved, order = pl.pallas_call(
         functools.partial(kernel, ntx, nty),
-        out_shape=jax.ShapeDtypeStruct(field.shape, jnp.float32),
-        in_specs=[any_space] * 5 + [pl.BlockSpec(memory_space=pltpu.VMEM)],
-        out_specs=any_space,
+        out_shape=(pltpu.VMEM(field.shape, f32), pltpu.SMEM((K, S), i32)),
+        in_specs=[in_hbm] * 6,
+        out_specs=(pl.BlockSpec(memory_space=pltpu.VMEM), pl.BlockSpec(memory_space=pltpu.SMEM)),
         scratch_shapes=[
-            pltpu.VMEM((S, XP, YP, Z), jnp.float32),
-            pltpu.VMEM((S, XP, YP, Z), jnp.float32),
-            pltpu.VMEM((S, B, B, Z), jnp.float32),
-            pltpu.VMEM(heat.shape[1:], jnp.float32),
-            pltpu.VMEM((nd, 8, Z), jnp.float32),
-            pltpu.VMEM((nd, 8, Z), jnp.float32),
-            pltpu.VMEM((B * B, Z), jnp.float32),
-            pltpu.SMEM((K * S,), jnp.int32),
-            pltpu.SMEM((K,), jnp.int32),
-            pltpu.SMEM(speed.shape, jnp.float32),
-            pltpu.VMEM((8, Z), jnp.int32),
-            pltpu.VMEM((4, 8, Z), jnp.int32),
-            pltpu.VMEM((2, 2, S, B, Z), jnp.float32),
-            pltpu.VMEM((2, 4, S, B, Z), jnp.float32),
-            pltpu.VMEM((4, 8, Z), jnp.int32),
-            pltpu.VMEM((4, 8, Z), jnp.float32),
-            pltpu.VMEM((8, Z), jnp.int32),
-            pltpu.VMEM((8, Z), jnp.float32),
-            pltpu.VMEM((8, Z), jnp.float32),
-            pltpu.VMEM((S, 8, Z), jnp.float32),
-            pltpu.SemaphoreType.DMA((5,)),
+            pltpu.VMEM((S, B, B, Z), f32),
+            pltpu.VMEM((S, XP, YP, Z), f32),
+            pltpu.VMEM((S, XP, YP, Z), f32),
+            pltpu.VMEM(heat.shape[1:], f32),
+            pltpu.VMEM((nd, 8, Z), f32),
+            pltpu.VMEM((nd, 8, Z), f32),
+            pltpu.VMEM((B * B, Z), f32),
+            pltpu.VMEM((S, B * B, 2 * Z), jnp.bfloat16),
+            pltpu.VMEM((S, 2 * Z, Z), jnp.bfloat16),
+            pltpu.SMEM(label.shape, i32),
+            pltpu.SMEM(count.shape, i32),
+            pltpu.SMEM(speed.shape, f32),
+            pltpu.VMEM((1, Z), i32),
+            pltpu.VMEM((8, Z), i32),
+            pltpu.VMEM((4, 8, Z), i32),
+            pltpu.VMEM((2, 2, S, B, Z), f32),
+            pltpu.VMEM((2, 4, S, B, Z), f32),
+            pltpu.VMEM((4, 8, Z), i32),
+            pltpu.VMEM((4, 8, Z), f32),
+            pltpu.VMEM((8, Z), f32),
+            pltpu.VMEM((S, 8, Z), f32),
+            pltpu.SemaphoreType.DMA((6,)),
             pltpu.SemaphoreType.DMA,
             pltpu.SemaphoreType.DMA,
             pltpu.SemaphoreType.DMA((12,)),
             pltpu.SemaphoreType.DMA((12,)),
             pltpu.SemaphoreType.DMA((12,)),
+        ],
+        compiler_params=pltpu.CompilerParams(
+            collective_id=0, has_side_effects=True, vmem_limit_bytes=59 * 2**20
+        ),
+        name="grains",
+    )(field, heat, label, count, speed, locator.reshape(1, Z))
+    return pl.pallas_call(
+        restore,
+        out_shape=jax.ShapeDtypeStruct(field.shape, f32),
+        in_specs=[pl.BlockSpec(memory_space=pltpu.SMEM), pl.BlockSpec(memory_space=pltpu.VMEM)],
+        out_specs=in_hbm,
+        scratch_shapes=[
+            pltpu.VMEM(field.shape, f32),
             pltpu.SemaphoreType.DMA,
         ],
-        compiler_params=pltpu.CompilerParams(
-            collective_id=0, has_side_effects=True, vmem_limit_bytes=60 * 2**20
-        ),
-        name="grains",
-    )(
-        field,
-        heat,
-        label.reshape(K * S),
-        count.reshape(K),
-        speed,
-        locator.reshape(1, Z),
-    )
+        compiler_params=pltpu.CompilerParams(vmem_limit_bytes=32 * 2**20),
+        name="restore",
+    )(order, moved)
 
 
 def solution(mesh):

time: 45.4 us -> 36.4 us (0.80)
  local copies, waits for them, and re-layouts: 5.91 us -> 0 us
  Pallas kernels: 39.3 us -> 36.3 us
    unnamed x1 -> x0, local copies, waits for them, and re-layouts: 4.64 us -> none
    pallas_call x1 -> x2, Pallas kernels: 39.3 us -> 36.3 us  [the longest x1 34.2 us: on_device(): pl.pallas_call(functools.partial(kernel, ntx, nty), out_shape=(pltpu.VMEM...]
    reshape x1 -> x0, local copies, waits for them, and re-layouts: 1.27 us -> none  [on_device(): label.reshape(K * S)]
where the time goes in v2:
time: 36.4 us; the launch traced here: 36.3 us
  Pallas kernels  36.3 us (100%)
    pallas_call x1, Pallas kernels, on_device(): pl.pallas_call(functools.partial(kernel, ntx, nty), out_shape=(pltpu.VMEM...  34.2 us
    pallas_call x1, Pallas kernels, on_device(): pl.pallas_call(restore, out_shape=jax.ShapeDtypeStruct(field.shape, f32),...  2.08 us

profile of v2, /device:TPU:1, one launch (start us, length us, event | category | flops | bytes accessed | tf_op | source)
XLA Modules:
  0.0 36.3 jit_solution(8584335721131619220)
XLA Ops:
  0.0 34.2 %grains.1 = (f32[8,32,32,128]{3,2,1,0:T(8,128)S(1)}, s32[4,8]{1,0:T(4,128)S(4)}) custom-call(f32[8,32,32,128]{3,2,1,0:T(8,128)} %field_hbm.1, f32[1,512,256]{2,1,0:T(8,128)} %slab_hbm.1, s32[1,1,4,8]{3,2,1,0:T(4,128)} %label_hbm.1, s32[1,1,4]{2,1,0:T(1,128)} %count_hbm.1, f32[8192]{0:T(1024)} %speed_hbm.1, s32[1,128]{1,0:T(1,128)} %bitcast.1), custom_call_target="tpu_custom_call" | custom-call | tf_op jit(solution)/shard_map/grains/pallas_call | solution.py:442
  34.3 2.1 %restore.1 = f32[8,32,32,128]{3,2,1,0:T(8,128)} custom-call(s32[4,8]{1,0:T(4,128)S(4)} %get-tuple-element.7.order, f32[8,32,32,128]{3,2,1,0:T(8,128)S(1)} %get-tuple-element.8.moved), custom_call_target="tpu_custom_call" | custom-call | tf_op jit(solution)/shard_map/restore/pallas_call | solution.py:481

commit v3 on v2

--- a/solution.py
+++ b/solution.py
@@ -95,18 +95,83 @@
 
     lax.fori_loop(0, ntx, patches, 0)
     recv[me] = send[me]
+
+    lower_x, upper_x = jnp.maximum(tx - 1, 0), jnp.minimum(tx + 1, ntx - 1)
+    lower_y, upper_y = jnp.maximum(ty - 1, 0), jnp.minimum(ty + 1, nty - 1)
+    at_end = (tx == 0, tx == ntx - 1, ty == 0, ty == nty - 1)
+    target = ((lower_x, ty), (upper_x, ty), (tx, lower_y), (tx, upper_y))
+
+    def face(step, f):
+        if f >= 2:
+            return face_y.at[step, f - 2]
+        if step == 0:
+            return field_hbm.at[:, (0, B - 1)[f]]
+        return g1.at[:, (1, B)[f], pl.ds(8, B), :]
+
+    def to_peer(step, f):
+        if step == 2:
+            source, here, there = code, code_in.at[f], code_in.at[f ^ 1]
+        else:
+            source, here, there = face(step, f), face_in.at[step, f], face_in.at[step, f ^ 1]
+        sem = step * 4 + f
+        remote = functools.partial(
+            pltpu.make_async_remote_copy,
+            source, there, send_sem.at[sem], recv_sem.at[sem ^ 1], device_id=target[f], device_id_type=MESH,
+        )
+        local = functools.partial(pltpu.make_async_copy, source, here, own_sem.at[sem])
+        return remote, local
+
+    def begin(step, f):
+        remote, local = to_peer(step, f)
+
+        @pl.when(jnp.logical_not(at_end[f]))
+        def _():
+            remote().start()
+
+        @pl.when(at_end[f])
+        def _():
+            local().start()
+
+    def finish(step, f):
+        remote, local = to_peer(step, f)
+        back, _ = to_peer(step, f ^ 1)
+
+        @pl.when(jnp.logical_not(at_end[f]))
+        def _():
+            remote().wait_send()
+            back().wait_recv()
+
+        @pl.when(at_end[f])
+        def _():
+            local().wait()
+
+    loads[1].wait()
+    flat_raw = raw.reshape(S * B * B, Z)
+
+    def pack_raw(s, carry):
+        for side, row in ((0, 0), (1, B - 1)):
+            values = [flat_raw[pl.ds((s * B + x) * B + row, 8, stride=B), :] for x in range(0, B, 8)]
+            for x in range(0, B, 8):
+                face_y[0, side, s, pl.ds(x, 8), :] = values[x // 8]
+        return carry
+
+    lax.fori_loop(0, S, pack_raw, 0)
     pl.semaphore_wait(barrier, nd - 1)
     peers(
         lambda px, py: pltpu.make_async_remote_copy(
             send.at[px * nty + py], recv.at[me], heat_send, heat_recv, device_id=(px, py), device_id_type=MESH
         ).start()
     )
+    begin(0, 2)
+    begin(0, 3)
+    begin(0, 0)
+    begin(0, 1)
 
     loads[2].wait()
     loads[3].wait()
     loads[4].wait()
     loads[5].wait()
-    codes, orders, matches = [], [], []
+    lives, codes, orders, matches = [], [], [], []
     for k in range(K):
         live = [jnp.where(s < count[0, 0, k], label[0, 0, k, s] + 1, 0) for s in range(S)]
         if k == 0:
@@ -140,17 +205,23 @@
         if k == 0:
             for j in range(S):
                 order_out[k, j] = j
+        lives.append(live)
         codes.append(code_at)
         orders.append(order)
         matches.append(matched)
     own_code = jnp.zeros((8, Z), jnp.int32)
+    listed = jnp.zeros((8, Z), jnp.int32)
     mobility = jnp.zeros((8, Z), jnp.float32)
     for k in range(K):
         for s in range(S):
             here = (sub == s) & (group == k)
             own_code = jnp.where(here, codes[k][s], own_code)
+            listed = jnp.where(here, lives[k][s], listed)
             mobility = jnp.where(here, speed[label[0, 0, k, orders[k][s]]], mobility)
-    code[...] = own_code
+    code[0] = listed
+    code[1] = own_code
+    for f in range(4):
+        begin(2, f)
     mob[...] = DT * mobility
     for s in range(S):
         mm[s] = jnp.broadcast_to(mob[pl.ds(s, 1), :], (8, Z))
@@ -185,10 +256,9 @@
             for x in (0, XP - 1):
                 for j in range(4):
                     g[s, x, pl.ds(8 + 8 * j, 8), :] = zero
-    loads[1].wait()
     wide_group = lax.broadcasted_iota(jnp.int32, (16, Z), 1) // B
     scale = [
-        jnp.where(jnp.broadcast_to(code[pl.ds(s, 1), :], (16, Z)) > 0, ROOT, 0.0) for s in range(S)
+        jnp.where(jnp.broadcast_to(code[1, pl.ds(s, 1), :], (16, Z)) > 0, ROOT, 0.0) for s in range(S)
     ]
 
     def keep_split(s, row, value):
@@ -197,82 +267,22 @@
         split[s, pl.ds(row, 16), pl.ds(Z, Z)] = (value - high.astype(jnp.float32)).astype(jnp.bfloat16)
 
     def place_field(x, carry):
+        values = []
         for s in range(S):
             for j in range(0, 4, 2):
                 rows = pl.ds(8 * j, 16)
                 value = raw[s, x, rows, :]
                 for k in range(1, K):
                     value = jnp.where(wide_group == k, raw[orders[k][s], x, rows, :], value)
-                value = value * scale[s]
+                values.append(value * scale[s])
+        for s in range(S):
+            for j in range(0, 4, 2):
+                value = values[2 * s + j // 2]
                 g0[s, x + 1, pl.ds(8 + 8 * j, 16), :] = value
                 keep_split(s, pl.multiple_of(x * B, B) + 8 * j, value)
         return carry
 
     lax.fori_loop(0, B, place_field, 0)
-
-    lower_x, upper_x = jnp.maximum(tx - 1, 0), jnp.minimum(tx + 1, ntx - 1)
-    lower_y, upper_y = jnp.maximum(ty - 1, 0), jnp.minimum(ty + 1, nty - 1)
-    at_end = (tx == 0, tx == ntx - 1, ty == 0, ty == nty - 1)
-    target = ((lower_x, ty), (upper_x, ty), (tx, lower_y), (tx, upper_y))
-
-    def pack_y(g, step):
-        flat = g.reshape(S * PLANE, Z)
-
-        def one(s, carry):
-            for side, row in ((0, 8), (1, 8 + B - 1)):
-                for x in range(0, B, 8):
-                    value = flat[pl.ds(s * PLANE + (x + 1) * YP + row, 8, stride=YP), :]
-                    face_y[step, side, s, pl.ds(x, 8), :] = value
-            return carry
-
-        lax.fori_loop(0, S, one, 0)
-
-    def face(g, step, f):
-        if f < 2:
-            return g.at[:, (1, B)[f], pl.ds(8, B), :]
-        return face_y.at[step, f - 2]
-
-    def exchange(g, step, f):
-        source, sem = face(g, step, f), step * 4 + f
-        remote = pltpu.make_async_remote_copy(
-            source, face_in.at[step, f ^ 1], send_sem.at[sem], recv_sem.at[sem ^ 1],
-            device_id=target[f], device_id_type=MESH,
-        )
-        local = pltpu.make_async_copy(source, face_in.at[step, f], own_sem.at[sem])
-        return remote, local
-
-    def exchange_code(f):
-        sem = 8 + f
-        remote = pltpu.make_async_remote_copy(
-            code, code_in.at[f ^ 1], send_sem.at[sem], recv_sem.at[sem ^ 1],
-            device_id=target[f], device_id_type=MESH,
-        )
-        local = pltpu.make_async_copy(code, code_in.at[f], own_sem.at[sem])
-        return remote, local
-
-    def begin(pair, f):
-        @pl.when(jnp.logical_not(at_end[f]))
-        def _():
-            pair[0].start()
-
-        @pl.when(at_end[f])
-        def _():
-            pair[1].start()
-
-    def finish(pair_sent, pair_got, f):
-        @pl.when(jnp.logical_not(at_end[f]))
-        def _():
-            pair_sent[0].wait_send()
-            pair_got[0].wait_recv()
-
-        @pl.when(at_end[f])
-        def _():
-            pair_sent[1].wait()
-
-    pack_y(g0, 0)
-    for f in range(4):
-        begin(exchange_code(f), f)
-        begin(exchange(g0, 0, f), f)
 
     def sweep(g, i, use):
         rows = pl.ds(pl.multiple_of(i * CHUNK * B, CHUNK * B), CHUNK * B)
@@ -309,39 +319,46 @@
 
     lax.fori_loop(0, B // CHUNK, first_sweep, 0)
 
+    own_now = code[1]
     for f in range(4):
-        finish(exchange_code(f), exchange_code(f ^ 1), f)
-        index = jnp.zeros((8, Z), jnp.int32)
-        value = jnp.zeros((8, Z), jnp.float32)
-        own_now = code[...]
-        for s in range(S):
-            other = jnp.broadcast_to(code_in[f, pl.ds(s, 1), :], (8, Z))
-            same = (other == own_now) & (own_now > 0)
-            index = jnp.where(same, s, index)
-            value = jnp.where(same, mob[...], value)
-        move[f] = index
-        weight[f] = value
-
-    def add_faces(g, base, stride_s, stride_x, first_x, first_y, step, factor, f):
-        finish(exchange(g, step, f), exchange(g, step, f ^ 1), f)
+        finish(2, f)
+        for step in range(2):
+            index = jnp.zeros((8, Z), jnp.int32)
+            value = jnp.zeros((8, Z), jnp.float32)
+            for s in range(S):
+                other = jnp.broadcast_to(code_in[f, step, pl.ds(s, 1), :], (8, Z))
+                same = (other == own_now) & (own_now > 0)
+                index = jnp.where(same, s, index)
+                value = jnp.where(same, (ROOT, 1.0)[step] * mob[...], value)
+            move[step, f] = index
+            weight[step, f] = value
+
+    def add_faces(base, stride_s, stride_x, first_x, first_y, step, f):
+        finish(step, f)
         flat = base.reshape(S * stride_s, Z)
         source = face_in.at[step, f].reshape(S * B, Z)
-        turn, gain = move[f], weight[f] * factor
-
-        def one(i, carry):
-            got = jnp.take_along_axis(source[pl.ds(i, 8, stride=B), :], turn, axis=0)
-            if f < 2:
-                row = (first_x + (0, B - 1)[f]) * stride_x + first_y + i
-            else:
-                row = (first_x + i) * stride_x + first_y + (0, B - 1)[f - 2]
-            at = (pl.ds(row, 8, stride=stride_s), slice(None))
-            flat[at] = flat[at] + gain * got
+        turn, gain = move[step, f], weight[step, f]
+
+        def eight(n, carry):
+            places, values = [], []
+            for i in range(8):
+                cell = 8 * n + i
+                got = jnp.take_along_axis(source[pl.ds(cell, 8, stride=B), :], turn, axis=0)
+                if f < 2:
+                    row = (first_x + (0, B - 1)[f]) * stride_x + first_y + cell
+                else:
+                    row = (first_x + cell) * stride_x + first_y + (0, B - 1)[f - 2]
+                at = (pl.ds(row, 8, stride=stride_s), slice(None))
+                places.append(at)
+                values.append(flat[at] + gain * got)
+            for at, value in zip(places, values):
+                flat[at] = value
             return carry
 
-        lax.fori_loop(0, B, one, 0, unroll=4)
+        lax.fori_loop(0, B // 8, eight, 0)
 
     for f in range(4):
-        add_faces(g0, g1, PLANE, YP, 1, 8, 0, 1.0, f)
+        add_faces(g1, PLANE, YP, 1, 8, 0, f)
 
     everyone = pltpu.make_async_remote_copy(
         send.at[pl.ds(0, nd - 1)], recv.at[pl.ds(0, nd - 1)], heat_send, heat_recv,
@@ -363,30 +380,49 @@
         for a in range(4):
             u_ref[pl.ds((8 * a + s) * B, B), :] = placed[a * B : (a + 1) * B]
 
-    def heat_term(x, pairs):
-        for j in pairs:
+    flat0, flat1 = g0.reshape(S * PLANE, Z), g1.reshape(S * PLANE, Z)
+
+    def heat_row(side, row):
+        def one(n, carry):
+            u = u_ref[pl.ds(n * 8 * B + row, 8, stride=B), :]
+            values = []
+            for s in range(S):
+                at = (pl.ds(s * PLANE + (n * 8 + 1) * YP + 8 + row, 8, stride=YP), slice(None))
+                own = flat0[at]
+                values.append(flat1[at] + (mm[s] * u) * (own * (ROOT - own)))
+            for s in range(S):
+                face_y[1, side, s, pl.ds(pl.multiple_of(n * 8, 8), 8), :] = values[s]
+            return carry
+
+        lax.fori_loop(0, B // 8, one, 0)
+
+    def heat_term(x):
+        for j in (0, 2):
             u = u_ref[pl.ds((x - 1) * B + 8 * j, 16), :]
+            values = []
             for s in range(S):
                 at = (s, x, pl.ds(8 + 8 * j, 16), slice(None))
                 own = g0[at]
                 gain = jnp.concatenate([mm[s], mm[s]], axis=0)
-                value = g1[at] + (gain * u) * (own * (ROOT - own))
-                g1[at] = value
-                keep_split(s, pl.multiple_of((x - 1) * B, B) + 8 * j, value)
-
-    heat_term(1, (0, 2))
-    heat_term(B, (0, 2))
-    for f in (0, 1):
-        begin(exchange(g1, 1, f), f)
+                values.append(g1[at] + (gain * u) * (own * (ROOT - own)))
+            for s in range(S):
+                g1[s, x, pl.ds(8 + 8 * j, 16), :] = values[s]
+                keep_split(s, pl.multiple_of((x - 1) * B, B) + 8 * j, values[s])
+
+    heat_row(0, 0)
+    begin(1, 2)
+    heat_row(1, B - 1)
+    begin(1, 3)
+    heat_term(1)
+    begin(1, 0)
+    heat_term(B)
+    begin(1, 1)
 
     def heat_rest(x, carry):
-        heat_term(x, (0, 2))
+        heat_term(x)
         return carry
 
     lax.fori_loop(2, B, heat_rest, 0)
-    pack_y(g1, 1)
-    for f in (2, 3):
-        begin(exchange(g1, 1, f), f)
 
     def second(x, j, own, squares, sums):
         u = u_ref[pl.ds((x - 1) * B + 8 * j, 8), :]
@@ -401,7 +437,7 @@
 
     lax.fori_loop(0, B // CHUNK, second_sweep, 0)
     for f in range(4):
-        add_faces(g1, out, B * B, B, 0, 0, 1, 1.0, f)
+        add_faces(out, B * B, B, 0, 0, 1, f)
 
 
 def restore(order, moved, result_hbm, result, out_sem):
@@ -458,12 +494,12 @@
             pltpu.SMEM(count.shape, i32),
             pltpu.SMEM(speed.shape, f32),
             pltpu.VMEM((1, Z), i32),
-            pltpu.VMEM((8, Z), i32),
-            pltpu.VMEM((4, 8, Z), i32),
+            pltpu.VMEM((2, 8, Z), i32),
+            pltpu.VMEM((4, 2, 8, Z), i32),
             pltpu.VMEM((2, 2, S, B, Z), f32),
             pltpu.VMEM((2, 4, S, B, Z), f32),
-            pltpu.VMEM((4, 8, Z), i32),
-            pltpu.VMEM((4, 8, Z), f32),
+            pltpu.VMEM((2, 4, 8, Z), i32),
+            pltpu.VMEM((2, 4, 8, Z), f32),
             pltpu.VMEM((8, Z), f32),
             pltpu.VMEM((S, 8, Z), f32),
             pltpu.SemaphoreType.DMA((6,)),

time: 36.4 us -> 35.5 us (0.975)
  Pallas kernels: 36.3 us -> 35.4 us
    pallas_call x1, Pallas kernels: 34.2 us -> 33.3 us  [on_device(): pl.pallas_call(functools.partial(kernel, ntx, nty), out_shape=(pltpu.VMEM...]
where the time goes in v3:
time: 35.5 us; the launch traced here: 35.4 us
  Pallas kernels  35.4 us (100%)
    pallas_call x1, Pallas kernels, on_device(): pl.pallas_call(functools.partial(kernel, ntx, nty), out_shape=(pltpu.VMEM...  33.3 us
    pallas_call x1, Pallas kernels, on_device(): pl.pallas_call(restore, out_shape=jax.ShapeDtypeStruct(field.shape, f32),...  2.08 us

profile of v3, /device:TPU:1, one launch (start us, length us, event | category | flops | bytes accessed | tf_op | source)
XLA Modules:
  0.0 35.4 jit_solution(7384458350989069580)
XLA Ops:
  0.0 33.3 %grains.1 = (f32[8,32,32,128]{3,2,1,0:T(8,128)S(1)}, s32[4,8]{1,0:T(4,128)S(4)}) custom-call(f32[8,32,32,128]{3,2,1,0:T(8,128)} %field_hbm.1, f32[1,512,256]{2,1,0:T(8,128)} %slab_hbm.1, s32[1,1,4,8]{3,2,1,0:T(4,128)} %label_hbm.1, s32[1,1,4]{2,1,0:T(1,128)} %count_hbm.1, f32[8192]{0:T(1024)} %speed_hbm.1, s32[1,128]{1,0:T(1,128)} %bitcast.1), custom_call_target="tpu_custom_call" | custom-call | tf_op jit(solution)/shard_map/grains/pallas_call | solution.py:478
  33.3 2.1 %restore.1 = f32[8,32,32,128]{3,2,1,0:T(8,128)} custom-call(s32[4,8]{1,0:T(4,128)S(4)} %get-tuple-element.7.order, f32[8,32,32,128]{3,2,1,0:T(8,128)S(1)} %get-tuple-element.8.moved), custom_call_target="tpu_custom_call" | custom-call | tf_op jit(solution)/shard_map/restore/pallas_call | solution.py:517

commit v4 on v3

--- a/solution.py
+++ b/solution.py
@@ -38,7 +38,7 @@
     label, count, speed, locator_ref,
     code, code_in, face_y, face_in,
     move, weight, mob, mm,
-    load_sem, heat_send, heat_recv, send_sem, recv_sem, own_sem,
+    all_in, load_sem, heat_send, heat_recv, send_sem, recv_sem, own_sem,
 ):
     nd = ntx * nty
     tx, ty = lax.axis_index("track"), lax.axis_index("cross")
@@ -59,22 +59,17 @@
     loads[0].start()
     barrier = pltpu.get_barrier_semaphore()
 
-    def peers(action):
-        def outer(i, carry):
-            px = lax.rem(tx + i, ntx)
-
-            def inner(j, carry):
-                @pl.when(i + j > 0)
-                def _():
-                    action(px, lax.rem(ty + j, nty))
-
-                return carry
-
-            return lax.fori_loop(0, nty, inner, carry)
-
-        lax.fori_loop(0, ntx, outer, 0)
-
-    peers(lambda px, py: pl.semaphore_signal(barrier, inc=1, device_id=(px, py), device_id_type=MESH))
+    def tell(axis, semaphore_at):
+        def one(i, carry):
+            px = lax.rem(tx + i, ntx) if axis == 0 else tx
+            py = lax.rem(ty + i, nty) if axis == 1 else ty
+            pl.semaphore_signal(semaphore_at(i), inc=1, device_id=(px, py), device_id_type=MESH)
+            return carry
+
+        lax.fori_loop(1, (ntx, nty)[axis], one, 0)
+
+    tell(1, lambda i: barrier)
+    tell(0, lambda i: barrier)
     for entry in loads[1:]:
         entry.start()
 
@@ -156,16 +151,30 @@
         return carry
 
     lax.fori_loop(0, S, pack_raw, 0)
-    pl.semaphore_wait(barrier, nd - 1)
-    peers(
-        lambda px, py: pltpu.make_async_remote_copy(
-            send.at[px * nty + py], recv.at[me], heat_send, heat_recv, device_id=(px, py), device_id_type=MESH
-        ).start()
-    )
+    pl.semaphore_wait(barrier, ntx + nty - 2)
+    tell(1, lambda i: all_in.at[i])
+
+    def to_row(py, first):
+        def one(i, carry):
+            px = lax.rem(tx + i, ntx)
+            pltpu.make_async_remote_copy(
+                send.at[px * nty + py], recv.at[me], heat_send, heat_recv, device_id=(px, py), device_id_type=MESH
+            ).start()
+            return carry
+
+        lax.fori_loop(first, ntx, one, 0)
+
+    def next_row(i, carry):
+        pl.semaphore_wait(all_in.at[i], 1)
+        to_row(lax.rem(ty + nty - i, nty), 0)
+        return carry
+
+    to_row(ty, 1)
     begin(0, 2)
     begin(0, 3)
     begin(0, 0)
     begin(0, 1)
+    lax.fori_loop(1, nty, next_row, 0)
 
     loads[2].wait()
     loads[3].wait()
@@ -502,6 +511,7 @@
             pltpu.VMEM((2, 4, 8, Z), f32),
             pltpu.VMEM((8, Z), f32),
             pltpu.VMEM((S, 8, Z), f32),
+            pltpu.SemaphoreType.REGULAR((nty,)),
             pltpu.SemaphoreType.DMA((6,)),
             pltpu.SemaphoreType.DMA,
             pltpu.SemaphoreType.DMA,

time: 35.5 us -> 31.8 us (0.90)
  Pallas kernels: 35.4 us -> 31.7 us
    pallas_call x1, Pallas kernels: 33.3 us -> 29.6 us  [on_device(): pl.pallas_call(functools.partial(kernel, ntx, nty), out_shape=(pltpu.VMEM...]
where the time goes in v4:
time: 31.8 us; the launch traced here: 31.7 us
  Pallas kernels  31.7 us (100%)
    pallas_call x1, Pallas kernels, on_device(): pl.pallas_call(functools.partial(kernel, ntx, nty), out_shape=(pltpu.VMEM...  29.6 us
    pallas_call x1, Pallas kernels, on_device(): pl.pallas_call(restore, out_shape=jax.ShapeDtypeStruct(field.shape, f32),...  2.08 us

profile of v4, /device:TPU:1, one launch (start us, length us, event | category | flops | bytes accessed | tf_op | source)
XLA Modules:
  0.0 31.7 jit_solution(12333719845108914104)
XLA Ops:
  0.0 29.6 %grains.1 = (f32[8,32,32,128]{3,2,1,0:T(8,128)S(1)}, s32[4,8]{1,0:T(4,128)S(4)}) custom-call(f32[8,32,32,128]{3,2,1,0:T(8,128)} %field_hbm.1, f32[1,512,256]{2,1,0:T(8,128)} %slab_hbm.1, s32[1,1,4,8]{3,2,1,0:T(4,128)} %label_hbm.1, s32[1,1,4]{2,1,0:T(1,128)} %count_hbm.1, f32[8192]{0:T(1024)} %speed_hbm.1, s32[1,128]{1,0:T(1,128)} %bitcast.1), custom_call_target="tpu_custom_call" | custom-call | tf_op jit(solution)/shard_map/grains/pallas_call | solution.py:487
  29.6 2.1 %restore.1 = f32[8,32,32,128]{3,2,1,0:T(8,128)} custom-call(s32[4,8]{1,0:T(4,128)S(4)} %get-tuple-element.7.order, f32[8,32,32,128]{3,2,1,0:T(8,128)S(1)} %get-tuple-element.8.moved), custom_call_target="tpu_custom_call" | custom-call | tf_op jit(solution)/shard_map/restore/pallas_call | solution.py:527

commit v5 on v4

--- a/solution.py
+++ b/solution.py
@@ -22,7 +22,7 @@
 XP = B + 2
 YP = B + 16
 PLANE = XP * YP
-PIECE = 2
+PIECE = 4
 CHUNK = 8
 
 
@@ -394,6 +394,8 @@
     def heat_row(side, row):
         def one(n, carry):
             u = u_ref[pl.ds(n * 8 * B + row, 8, stride=B), :]
+            done = (n * 8 + sub == 0) | (n * 8 + sub == B - 1)
+            u = jnp.where(done, 0.0, u)
             values = []
             for s in range(S):
                 at = (pl.ds(s * PLANE + (n * 8 + 1) * YP + 8 + row, 8, stride=YP), slice(None))
@@ -418,14 +420,14 @@
                 g1[s, x, pl.ds(8 + 8 * j, 16), :] = values[s]
                 keep_split(s, pl.multiple_of((x - 1) * B, B) + 8 * j, values[s])
 
+    heat_term(1)
+    begin(1, 0)
+    heat_term(B)
+    begin(1, 1)
     heat_row(0, 0)
     begin(1, 2)
     heat_row(1, B - 1)
     begin(1, 3)
-    heat_term(1)
-    begin(1, 0)
-    heat_term(B)
-    begin(1, 1)
 
     def heat_rest(x, carry):
         heat_term(x)

time: 31.8 us -> 31.7 us (level)
  no operation moved by 1% of the time
where the time goes in v5:
time: 31.7 us; the launch traced here: 31.6 us
  Pallas kernels  31.6 us (100%)
    pallas_call x1, Pallas kernels, on_device(): pl.pallas_call(functools.partial(kernel, ntx, nty), out_shape=(pltpu.VMEM...  29.5 us
    pallas_call x1, Pallas kernels, on_device(): pl.pallas_call(restore, out_shape=jax.ShapeDtypeStruct(field.shape, f32),...  2.14 us

profile of v5, /device:TPU:1, one launch (start us, length us, event | category | flops | bytes accessed | tf_op | source)
XLA Modules:
  0.0 31.6 jit_solution(6812732543890079012)
XLA Ops:
  0.0 29.5 %grains.1 = (f32[8,32,32,128]{3,2,1,0:T(8,128)S(1)}, s32[4,8]{1,0:T(4,128)S(4)}) custom-call(f32[8,32,32,128]{3,2,1,0:T(8,128)} %field_hbm.1, f32[1,512,256]{2,1,0:T(8,128)} %slab_hbm.1, s32[1,1,4,8]{3,2,1,0:T(4,128)} %label_hbm.1, s32[1,1,4]{2,1,0:T(1,128)} %count_hbm.1, f32[8192]{0:T(1024)} %speed_hbm.1, s32[1,128]{1,0:T(1,128)} %bitcast.1), custom_call_target="tpu_custom_call" | custom-call | tf_op jit(solution)/shard_map/grains/pallas_call | solution.py:489
  29.5 2.1 %restore.1 = f32[8,32,32,128]{3,2,1,0:T(8,128)} custom-call(s32[4,8]{1,0:T(4,128)S(4)} %get-tuple-element.7.order, f32[8,32,32,128]{3,2,1,0:T(8,128)S(1)} %get-tuple-element.8.moved), custom_call_target="tpu_custom_call" | custom-call | tf_op jit(solution)/shard_map/restore/pallas_call | solution.py:529
